TPU v7x, 32 devices: a whole 2x2x4 slice. The times are simulated.
32 devices in a mesh: rep: 8 (over z, x), tp: 4 (over y, core).
Axes of the slice: x: 2, y: 2, z: 4, core: 2. Of those that a mesh axis runs over, the one named last changes fastest.
Arguments:
- suffix_source: bfloat16 [8, 384, 4096], P('rep', None, 'tp'), may hold values from -6 to 6
- suffix_accept: bfloat16 [8, 384, 4096], P('rep', None, 'tp'), may hold values from -3 to 3
- suffix_address: bfloat16 [8, 384, 4096], P('rep', None, 'tp'), may hold values from -3 to 3
- guess_lane_source: bfloat16 [16, 16, 4096], P('rep', None, 'tp'), may hold values from -6 to 6
- guess_lane_accept: bfloat16 [16, 16, 4096], P('rep', None, 'tp'), may hold values from -3 to 3
- guess_lane_address: bfloat16 [16, 16, 4096], P('rep', None, 'tp'), may hold values from -3 to 3
- content_map: bfloat16 [4096, 4096], P(None, 'tp'), may hold values from -0.09375 to 0.09375
- forget_shrink_map: bfloat16 [4096, 128], replicated, may hold values from -0.09375 to 0.09375
- forget_expand_map: bfloat16 [128, 4096], P(None, 'tp'), may hold values from -0.35351562 to 0.35351562
- forget_lane_anchor: float32 [4096], P('tp'), may hold values from -12 to -3
- present_boost: float32 [4096], P('tp'), may hold values from -1.5 to 1.5
- content_blend_share: float32 [4096], P('tp'), may hold values from 0 to 1
- forget_blend_share: float32 [4096], P('tp'), may hold values from 0 to 1
- lane_normal_scale: float32 [4096], P('tp'), may hold values from 0.5 to 1.5
- lane_normal_shift: float32 [4096], P('tp'), may hold values from -1.2 to 1.2
- kernel_memory_saved: float32 [16, 64, 4096], P(None, 'rep', 'tp'), may hold values from -6 to 6
- prior_source_saved: bfloat16 [16, 64, 64], P(None, 'rep', 'tp'), may hold values from -6 to 6
- lane_owner: int32 [16], replicated, may hold values from 0 to 15, as said below
- request_spans: int32 [16], replicated, may hold values from 16 to 400, as said below
- admitted_guesses: int32 [16], replicated, may hold values from 0 to 16
Outputs:
- tail_out: bfloat16 [8, 384, 4096], P('rep', None, 'tp')
- draft_out: bfloat16 [16, 16, 4096], P('rep', None, 'tp')
- state_out: float32 [16, 64, 4096], P(None, 'rep', 'tp')
- shift_out: bfloat16 [16, 64, 64], P(None, 'rep', 'tp')
Inputs may be any that keep to these rules, and one draw needn't show every extreme that they name: `lane_owner`: a permutation of the request numbers. `request_spans`: exactly 1 request have 16 + 384 tokens and the others 16; a long request is always dealt to a slot s with s % 2 == 0; each aligned block of 8 consecutive groups holds exactly one group whose first slot is long; the tail buffers of groups whose first slot is not long are not read.
All inputs are finite; a program needn't handle non-finite values.
Results may differ from a plain program's by a relative error of at most 0.0051.
The roundings to bfloat16 on the way count: a program that leaves them out, or rounds other values in their place, can miss the bound.
Values may be sent and summed in bfloat16 or wider, within the bound.
No kernel may reach another device: no remote copies, remote signals or barrier semaphores. Data moves between devices by JAX's collectives and lax.ppermute only.
A program may use at most 128 MiB of HBM per device.

v0:
```python
import jax
import jax.numpy as jnp
from jax import lax
from jax.sharding import PartitionSpec as P

SUBSPACE_SPAN = 64
DRAFT = 16


HIGH = lax.Precision.HIGHEST
EPS = 0.00064


def group_norm(answer_collection, lane_normal_scale, lane_normal_shift):
    center = answer_collection - jnp.mean(answer_collection, axis=-1, keepdims=True)
    spread = jnp.mean(center * center, axis=-1, keepdims=True)
    normed = (center / jnp.sqrt(spread + EPS)).reshape(answer_collection.shape[0], -1)
    return (normed * lane_normal_scale + lane_normal_shift).astype(jnp.bfloat16)


def token_mix(current, previous, mixing):
    present = current.astype(jnp.float32)
    return (present + (previous.astype(jnp.float32) - present) * mixing).astype(jnp.bfloat16)


def project(
    mixed_value,
    decay_mixed_input,
    content_map,
    forget_shrink_map,
    forget_expand_map,
    forget_lane_anchor,
):
    acc_value = jnp.dot(
        lax.all_gather(mixed_value, "tp", axis=1, tiled=True),
        content_map,
        preferred_element_type=jnp.float32,
    )
    decay_accumulated = jnp.dot(
        lax.all_gather(decay_mixed_input, "tp", axis=1, tiled=True),
        forget_shrink_map,
        preferred_element_type=jnp.float32,
    )
    acc_value, decay_accumulated = (acc_value, decay_accumulated)
    content_vectors = acc_value.astype(jnp.bfloat16)
    decay_low_rank = jnp.tanh(decay_accumulated).astype(jnp.bfloat16)
    forget_logscale = -jnp.exp(
        forget_lane_anchor
        + jnp.dot(decay_low_rank, forget_expand_map, preferred_element_type=jnp.float32)
    )
    return (content_vectors, forget_logscale)


def process_blocks(
    accept_vectors, address_vectors, content_vectors, forget_logscale, ongoing_memory, lanes_boost
):
    total_steps = accept_vectors.shape[0]
    block_len = min(64, total_steps)
    block_count = total_steps // block_len
    lower = jnp.arange(block_len)[:, None] > jnp.arange(block_len)[None, :]

    def shape_blocks(array):
        return array.reshape(block_count, block_len, array.shape[1], array.shape[2])

    def one_block(threaded_pair, source_vectors):
        accept_vectors_all, address_vectors_all, value_rows_batch, rate_b = source_vectors
        inclusive = jnp.cumsum(rate_b, axis=0)
        exclusive = inclusive - rate_b
        middle = inclusive[block_len // 2]
        recept_scaled = accept_vectors_all * jnp.exp(exclusive - middle)
        keys_scaled = address_vectors_all * jnp.exp(middle - inclusive)
        scores = jnp.einsum("thi,shi->hts", recept_scaled, keys_scaled, precision=HIGH)
        scores = jnp.where(lower[None], scores, 0.0)
        answer_vectors = jnp.einsum("hts,shj->thj", scores, value_rows_batch, precision=HIGH)
        answer_vectors = answer_vectors + jnp.einsum(
            "thi,hij->thj", accept_vectors_all * jnp.exp(exclusive), threaded_pair, precision=HIGH
        )
        answer_vectors = (
            answer_vectors
            + jnp.sum(
                accept_vectors_all * lanes_boost * address_vectors_all, axis=-1, keepdims=True
            )
            * value_rows_batch
        )
        total = inclusive[-1]
        threaded_pair = jnp.exp(total)[:, :, None] * threaded_pair + jnp.einsum(
            "shi,shj->hij",
            address_vectors_all * jnp.exp(total - inclusive),
            value_rows_batch,
            precision=HIGH,
        )
        return (threaded_pair, answer_vectors)

    closing_answer, answer_collection = lax.scan(
        one_block,
        ongoing_memory,
        (
            shape_blocks(accept_vectors),
            shape_blocks(address_vectors),
            shape_blocks(content_vectors),
            shape_blocks(forget_logscale),
        ),
    )
    return (
        answer_collection.reshape(total_steps, accept_vectors.shape[1], accept_vectors.shape[2]),
        closing_answer,
    )


def local(
    suffix_source,
    suffix_accept,
    suffix_address,
    guess_lane_source,
    guess_lane_accept,
    guess_lane_address,
    content_map,
    forget_shrink_map,
    forget_expand_map,
    forget_lane_anchor,
    present_boost,
    content_blend_share,
    forget_blend_share,
    lane_normal_scale,
    lane_normal_shift,
    kernel_memory_saved,
    prior_source_saved,
    lane_owner,
    request_spans,
    admitted_guesses,
):
    local_width = content_map.shape[1]
    lanes_owned = local_width // SUBSPACE_SPAN
    slots = guess_lane_source.shape[0]
    squad_index = lax.axis_index("rep")
    slot_ids = squad_index * slots + jnp.arange(slots, dtype=jnp.int32)
    my_reqs = lane_owner[slot_ids]
    slot_long = request_spans[my_reqs] > DRAFT
    group_long = slot_long[0]
    lanes_boost = present_boost.reshape(lanes_owned, SUBSPACE_SPAN)
    ordered_state = kernel_memory_saved[lane_owner]
    ordered_shift = prior_source_saved[lane_owner].astype(jnp.float32)
    got_state, got_shift = (
        lax.all_to_all(ordered_state, "rep", split_axis=0, concat_axis=1, tiled=True),
        lax.all_to_all(ordered_shift, "rep", split_axis=0, concat_axis=1, tiled=True),
    )
    start = got_state.reshape(slots, SUBSPACE_SPAN, lanes_owned, SUBSPACE_SPAN).transpose(
        0, 2, 1, 3
    )
    start_prev = got_shift.astype(jnp.bfloat16).transpose(0, 2, 1).reshape(slots, local_width)

    def divide_lanes(array):
        return array.astype(jnp.float32).reshape(array.shape[0], lanes_owned, SUBSPACE_SPAN)

    tail_tokens = suffix_source[0]
    tail_len = tail_tokens.shape[0]
    tail_prev = jnp.concatenate([start_prev[:1], tail_tokens[:-1]], axis=0)
    tail_value = token_mix(tail_tokens, tail_prev, content_blend_share)
    tail_decay = token_mix(tail_tokens, tail_prev, forget_blend_share)
    tail_recept = suffix_accept[0]
    tail_keys = suffix_address[0]
    first = jnp.where(slot_long[:, None], tail_tokens[-1][None, :], start_prev)
    draft_prev = jnp.concatenate([first[:, None], guess_lane_source[:, :-1]], axis=1)
    draft_value = token_mix(guess_lane_source, draft_prev, content_blend_share).reshape(
        slots * DRAFT, local_width
    )
    draft_decay = token_mix(guess_lane_source, draft_prev, forget_blend_share).reshape(
        slots * DRAFT, local_width
    )
    content_vectors, forget_logscale = project(
        jnp.concatenate([tail_value, draft_value], axis=0),
        jnp.concatenate([tail_decay, draft_decay], axis=0),
        content_map,
        forget_shrink_map,
        forget_expand_map,
        forget_lane_anchor,
    )
    tail_y, tail_end = process_blocks(
        divide_lanes(tail_recept),
        divide_lanes(tail_keys),
        divide_lanes(content_vectors[:tail_len]),
        forget_logscale[:tail_len].reshape(tail_len, lanes_owned, SUBSPACE_SPAN),
        start[0],
        lanes_boost,
    )
    tail_norm = group_norm(tail_y, lane_normal_scale, lane_normal_shift)
    tail_out = jnp.where(group_long, tail_norm, jnp.zeros_like(tail_norm))[None]
    guess_content = (
        content_vectors[tail_len:]
        .astype(jnp.float32)
        .reshape(slots, DRAFT, lanes_owned, SUBSPACE_SPAN)
    )
    guess_forget = forget_logscale[tail_len:].reshape(slots, DRAFT, lanes_owned, SUBSPACE_SPAN)
    guess_accept = guess_lane_accept.astype(jnp.float32).reshape(
        slots, DRAFT, lanes_owned, SUBSPACE_SPAN
    )
    guess_address = guess_lane_address.astype(jnp.float32).reshape(
        slots, DRAFT, lanes_owned, SUBSPACE_SPAN
    )
    trailing_pair = jnp.where(slot_long[:, None, None, None], tail_end[None], start)
    draft_y, draft_final = jax.vmap(process_blocks, in_axes=(0, 0, 0, 0, 0, None))(
        guess_accept, guess_address, guess_content, guess_forget, trailing_pair, lanes_boost
    )
    draft_out = group_norm(
        draft_y.reshape(slots * DRAFT, lanes_owned, SUBSPACE_SPAN),
        lane_normal_scale,
        lane_normal_shift,
    ).reshape(slots, DRAFT, local_width)
    count = admitted_guesses[my_reqs]
    taken = jnp.arange(DRAFT, dtype=jnp.int32)[None, :] < count[:, None]
    inclusive_d = jnp.cumsum(guess_forget, axis=1)
    upto = jnp.sum(jnp.where(taken[:, :, None, None], guess_forget, 0.0), axis=1)
    weight = jnp.where(taken[:, :, None, None], jnp.exp(upto[:, None] - inclusive_d), 0.0)
    chosen = jnp.exp(upto)[..., None] * trailing_pair + jnp.einsum(
        "sthi,sthj->shij", guess_address * weight, guess_content, precision=HIGH
    )
    edge_row = guess_lane_source[jnp.arange(slots), jnp.maximum(count - 1, 0)]
    edge = jnp.where((count > 0)[:, None], edge_row, first)
    ret_state = chosen.transpose(0, 2, 1, 3).reshape(slots, SUBSPACE_SPAN, local_width)
    ret_shift = (
        edge.reshape(slots, lanes_owned, SUBSPACE_SPAN).transpose(0, 2, 1).astype(jnp.float32)
    )
    back_state, back_shift = (
        lax.all_to_all(ret_state, "rep", split_axis=1, concat_axis=0, tiled=True),
        lax.all_to_all(ret_shift, "rep", split_axis=1, concat_axis=0, tiled=True),
    )
    total_reqs = lane_owner.shape[0]
    inverse = (
        jnp.zeros((total_reqs,), jnp.int32)
        .at[lane_owner]
        .set(jnp.arange(total_reqs, dtype=jnp.int32))
    )
    state_out = back_state[inverse]
    shift_out = back_shift[inverse].astype(jnp.bfloat16)
    return (tail_out, draft_out, state_out, shift_out)


def solution(mesh):
    placed = (
        P("rep", None, "tp"),
        P("rep", None, "tp"),
        P("rep", None, "tp"),
        P("rep", None, "tp"),
        P("rep", None, "tp"),
        P("rep", None, "tp"),
        P(None, "tp"),
        P(),
        P(None, "tp"),
        P("tp"),
        P("tp"),
        P("tp"),
        P("tp"),
        P("tp"),
        P("tp"),
        P(None, "rep", "tp"),
        P(None, "rep", "tp"),
        P(),
        P(),
        P(),
    )
    return jax.shard_map(
        local,
        mesh=mesh,
        in_specs=placed,
        out_specs=(
            P("rep", None, "tp"),
            P("rep", None, "tp"),
            P(None, "rep", "tp"),
            P(None, "rep", "tp"),
        ),
        check_vma=False,
    )
```

profile of v0, /device:TPU:0, one launch (start us, length us, event | category | flops | bytes accessed | tf_op | source)
XLA Modules:
  0.0 207.5 jit_solution(13322176341247680399)
XLA Ops:
  8.5 1.3 gather_fusion.3
  10.5 7.3 %all-to-all-start.1 = ((bf16[8,2,128]{2,1,0:T(2,128)(2,1)}), bf16[8,2,128]{2,1,0:T(2,128)(2,1)S(1)}, u32[]{:S(2)}, u32[]{:S(2)}) async-start(bf16[8,2,128]{2,1,0:T(2,128)(2,1)} %reshape.474), calls=%async_computation.1 | async-start | bytes 8192 | tf_op jit(solution)/shard_map/all_to_all | solution.py:145
  17.9 1.3 gather_fusion
  19.2 1.3 gather_fusion.4
  20.5 1.3 gather_fusion.1
  21.9 2.2 %all-to-all-done.1 = bf16[8,2,128]{2,1,0:T(2,128)(2,1)S(1)} async-done(((bf16[8,2,128]{2,1,0:T(2,128)(2,1)}), bf16[8,2,128]{2,1,0:T(2,128)(2,1)S(1)}, u32[]{:S(2)}, u32[]{:S(2)}) %all-to-all-start.1) | async-done | bytes 4128 | tf_op jit(solution)/shard_map/all_to_all | solution.py:145
  29.9 3.7 %all-to-all-start.3 = ((bf16[8,2,128]{2,1,0:T(2,128)(2,1)}), bf16[8,2,128]{2,1,0:T(2,128)(2,1)S(1)}, u32[]{:S(2)}, u32[]{:S(2)}) async-start(bf16[8,2,128]{2,1,0:T(2,128)(2,1)} %reshape.476), calls=%async_computation.3 | async-start | bytes 8192 | tf_op jit(solution)/shard_map/all_to_all | solution.py:225
  33.6 1.4 gather_fusion.2
  35.0 5.0 %all-to-all-done.3 = bf16[8,2,128]{2,1,0:T(2,128)(2,1)S(1)} async-done(((bf16[8,2,128]{2,1,0:T(2,128)(2,1)}), bf16[8,2,128]{2,1,0:T(2,128)(2,1)S(1)}, u32[]{:S(2)}, u32[]{:S(2)}) %all-to-all-start.3) | async-done | bytes 4128 | tf_op jit(solution)/shard_map/all_to_all | solution.py:225
  40.0 3.5 %all-to-all-start = ((f32[16,8,1024]{2,1,0:T(8,128)}), f32[16,8,1024]{2,1,0:T(8,128)S(1)}, u32[]{:S(2)}, u32[]{:S(2)}) async-start(f32[16,8,1024]{2,1,0:T(8,128)} %gather_fusion.2), calls=%async_computation | async-start | bytes 1048576 | tf_op jit(solution)/shard_map/all_to_all | solution.py:144
  46.0 2.2 %reshape.386 = f32[6,64,16,64]{3,2,1,0:T(8,128)} reshape(bf16[1,384,1024]{2,1,0:T(8,128)(2,1)S(1)} %copy-done.13) | data formatting | bytes 2359296 | tf_op jit(solution)/shard_map/convert_element_type | solution.py:153
  48.2 2.1 %reshape.384 = f32[6,64,16,64]{3,2,1,0:T(8,128)} reshape(bf16[1,384,1024]{2,1,0:T(8,128)(2,1)S(1)} %copy-done.14) | data formatting | bytes 2359296 | tf_op jit(solution)/shard_map/convert_element_type | solution.py:153
  51.6 1.2 gather_fusion.7
  52.8 3.4 %all-to-all-done = f32[16,8,1024]{2,1,0:T(8,128)S(1)} async-done(((f32[16,8,1024]{2,1,0:T(8,128)}), f32[16,8,1024]{2,1,0:T(8,128)S(1)}, u32[]{:S(2)}, u32[]{:S(2)}) %all-to-all-start) | async-done | bytes 524320 | tf_op jit(solution)/shard_map/all_to_all | solution.py:144
  57.8 8.1 %convolution_convert_fusion = bf16[416,1024]{1,0:T(8,128)(2,1)S(1)} fusion(bf16[416,4096]{1,0:T(8,128)(2,1)} %all-gather.5.cloned.1.call-done, bf16[4096,1024]{1,0:T(8,128)(2,1)} %param.28), kind=kOutput, calls=%fused_computation.48 | convolution fusion | flops 3490086912 | bytes 12648448 | tf_op jit(solution)/shard_map/dot_general | solution.py:34
  66.5 1.3 slice_convert_fusion
  67.9 20.1 %all-gather.3.cloned.1.call-done = bf16[416,4096]{1,0:T(8,128)(2,1)} async-done(((bf16[416,1024]{1,0:T(8,128)(2,1)}), bf16[416,4096]{1,0:T(8,128)(2,1)}) %all-gather.3.cloned.1.call-update) | async-done | bytes 3407888 | tf_op jit(solution)/shard_map/all_gather | solution.py:40
  88.0 3.7 %exponential_negate_fusion = f32[416,1024]{1,0:T(8,128)S(1)} fusion(bf16[128,1024]{1,0:T(8,128)(2,1)S(1)} %copy-done.17, bf16[416,4096]{1,0:T(8,128)(2,1)} %all-gather.3.cloned.1.call-done, bf16[4096,128]{1,0:T(8,128)(2,1)S(1)} %copy-done, f32[1024]{0:T(1024)} %param.31), kind=kOutput, calls=%fused_computation.44 | convolution fusion | flops 546164736 | bytes 6426624 | tf_op jit(solution)/shard_map/dot_general | solution.py:49
  91.7 1.1 copy-done.5
  93.1 1.4 fusion.41
  94.7 1.1 select_multiply_fusion
  95.9 2.1 %reshape_reshape.7 = f32[6,64,16,64]{3,2,1,0:T(8,128)} reshape(f32[384,1024]{1,0:T(8,128)S(1)} %slice-done) | data formatting | bytes 3145728 | tf_op jit(solution)/shard_map/reshape;reshape | solution.py:63
  98.0 3.4 %reshape.385 = f32[6,64,16,64]{3,2,1,0:T(8,128)} reshape(f32[384,1024]{1,0:T(8,128)} %slice_convert_fusion) | data formatting | bytes 3145728 | tf_op jit(solution)/shard_map/reshape;reshape | solution.py:63
  101.5 60.3 %while.3 = (s32[]{:T(128)}, f32[16,64,64]{2,1,0:T(8,128)S(1)}, f32[6,64,16,64]{3,1,2,0:T(8,128)}, f32[6,64,16,64]{3,2,1,0:T(8,128)}, f32[6,64,16,64]{3,2,1,0:T(8...) while((s32[]{:T(128)}, f32[16,64,64]{2,1,0:T(8,128)S(1)}, ...), condition=%wide.region_3.4_spmd.clone, body=%wide.region_0.3_spmd.clone.sunk | while | flops 206572544 | bytes 8724625 | solution.py:94
  102.6 1.1 fusion.68
  103.8 2.5 %bitcast_multiply_fusion.6 = (f32[64,16,64]{2,1,0:T(8,128)S(1)}, f32[64,16,64]{2,1,0:T(8,128)S(1)}, f32[64,16]{1,0:T(8,128)S(1)}, f32[64,16,64]{2,1,0:T(8,128)S(1)}, f32[64,16,64]{2,1,0:T(8,128)}) fusion(f32[64,16,64]{2,1,0:T(8,128)S(1)} %fusion.68, f32[6,64,16,64]{3,2,1,0:T(8,128)} %get-tuple-element.268, s32[]{:T(128)S(6)} %copy.263, ...), kind=kLoop, calls=%fused_computation.24.clone.1 | loop fusion | flops 719872 | bytes 2113540 | tf_op jit(solution)/shard_map/while/body/eval_jaxpr/mul | solution.py:71
  106.3 1.3 convolution_select_fusion.3
  108.4 1.8 fusion.70
  110.2 1.3 convolution_add_fusion.3
  112.7 1.1 fusion.68
  113.8 2.5 %bitcast_multiply_fusion.6 = (f32[64,16,64]{2,1,0:T(8,128)S(1)}, f32[64,16,64]{2,1,0:T(8,128)S(1)}, f32[64,16]{1,0:T(8,128)S(1)}, f32[64,16,64]{2,1,0:T(8,128)S(1)}, f32[64,16,64]{2,1,0:T(8,128)}) fusion(f32[64,16,64]{2,1,0:T(8,128)S(1)} %fusion.68, f32[6,64,16,64]{3,2,1,0:T(8,128)} %get-tuple-element.268, s32[]{:T(128)S(6)} %copy.263, ...), kind=kLoop, calls=%fused_computation.24.clone.1 | loop fusion | flops 719872 | bytes 2113540 | tf_op jit(solution)/shard_map/while/body/eval_jaxpr/mul | solution.py:71
  116.4 1.3 convolution_select_fusion.3
  118.5 1.8 fusion.70
  120.3 1.3 convolution_add_fusion.3
  122.8 1.1 fusion.68
  123.9 2.5 %bitcast_multiply_fusion.6 = (f32[64,16,64]{2,1,0:T(8,128)S(1)}, f32[64,16,64]{2,1,0:T(8,128)S(1)}, f32[64,16]{1,0:T(8,128)S(1)}, f32[64,16,64]{2,1,0:T(8,128)S(1)}, f32[64,16,64]{2,1,0:T(8,128)}) fusion(f32[64,16,64]{2,1,0:T(8,128)S(1)} %fusion.68, f32[6,64,16,64]{3,2,1,0:T(8,128)} %get-tuple-element.268, s32[]{:T(128)S(6)} %copy.263, ...), kind=kLoop, calls=%fused_computation.24.clone.1 | loop fusion | flops 719872 | bytes 2113540 | tf_op jit(solution)/shard_map/while/body/eval_jaxpr/mul | solution.py:71
  126.5 1.3 convolution_select_fusion.3
  128.5 1.8 fusion.70
  130.3 1.3 convolution_add_fusion.3
  132.8 1.1 fusion.68
  134.0 2.5 %bitcast_multiply_fusion.6 = (f32[64,16,64]{2,1,0:T(8,128)S(1)}, f32[64,16,64]{2,1,0:T(8,128)S(1)}, f32[64,16]{1,0:T(8,128)S(1)}, f32[64,16,64]{2,1,0:T(8,128)S(1)}, f32[64,16,64]{2,1,0:T(8,128)}) fusion(f32[64,16,64]{2,1,0:T(8,128)S(1)} %fusion.68, f32[6,64,16,64]{3,2,1,0:T(8,128)} %get-tuple-element.268, s32[]{:T(128)S(6)} %copy.263, ...), kind=kLoop, calls=%fused_computation.24.clone.1 | loop fusion | flops 719872 | bytes 2113540 | tf_op jit(solution)/shard_map/while/body/eval_jaxpr/mul | solution.py:71
  136.5 1.3 convolution_select_fusion.3
  138.6 1.8 fusion.70
  140.4 1.3 convolution_add_fusion.3
  144.0 2.5 %bitcast_multiply_fusion.6 = (f32[64,16,64]{2,1,0:T(8,128)S(1)}, f32[64,16,64]{2,1,0:T(8,128)S(1)}, f32[64,16]{1,0:T(8,128)S(1)}, f32[64,16,64]{2,1,0:T(8,128)S(1)}, f32[64,16,64]{2,1,0:T(8,128)}) fusion(f32[64,16,64]{2,1,0:T(8,128)S(1)} %fusion.68, f32[6,64,16,64]{3,2,1,0:T(8,128)} %get-tuple-element.268, s32[]{:T(128)S(6)} %copy.263, ...), kind=kLoop, calls=%fused_computation.24.clone.1 | loop fusion | flops 719872 | bytes 2113540 | tf_op jit(solution)/shard_map/while/body/eval_jaxpr/mul | solution.py:71
  146.6 1.3 convolution_select_fusion.3
  148.7 1.8 fusion.70
  150.4 1.3 convolution_add_fusion.3
  154.1 2.5 %bitcast_multiply_fusion.6 = (f32[64,16,64]{2,1,0:T(8,128)S(1)}, f32[64,16,64]{2,1,0:T(8,128)S(1)}, f32[64,16]{1,0:T(8,128)S(1)}, f32[64,16,64]{2,1,0:T(8,128)S(1)}, f32[64,16,64]{2,1,0:T(8,128)}) fusion(f32[64,16,64]{2,1,0:T(8,128)S(1)} %fusion.68, f32[6,64,16,64]{3,2,1,0:T(8,128)} %get-tuple-element.268, s32[]{:T(128)S(6)} %copy.263, ...), kind=kLoop, calls=%fused_computation.24.clone.1 | loop fusion | flops 719872 | bytes 2113540 | tf_op jit(solution)/shard_map/while/body/eval_jaxpr/mul | solution.py:71
  156.6 1.3 convolution_select_fusion.3
  158.7 1.8 fusion.70
  160.5 1.3 convolution_add_fusion.3
  161.8 2.8 %reduce_sum.64 = f32[6,64,16]{1,2,0:T(8,128)S(1)} reduce(f32[6,64,16,64]{3,1,2,0:T(8,128)} %get-tuple-element.79, f32[]{:T(128)} %constant.67.clone.1), dimensions={3}, to_apply=%region_4.5 | reduce | flops 387072 | bytes 1597444 | tf_op jit(solution)/shard_map/reduce_sum | solution.py:15
  164.6 3.3 %multiply_reduce_fusion = f32[6,64,16]{1,2,0:T(8,128)S(1)} fusion(f32[6,64,16,64]{3,1,2,0:T(8,128)} %get-tuple-element.79, f32[6,64,16]{1,2,0:T(8,128)S(1)} %broadcast_multiply_fusion), kind=kLoop, calls=%fused_computation.40 | loop fusion | flops 1173504 | bytes 1622016 | tf_op jit(solution)/shard_map/reduce_sum | solution.py:16
  168.9 1.3 fusion.24
  171.4 1.4 fusion.19
  173.4 1.3 reshape.469
  174.7 5.7 %all-to-all-start.2 = ((f32[2,64,1024]{2,0,1:T(2,128)}), f32[2,64,1024]{2,0,1:T(2,128)S(1)}, u32[]{:S(2)}, u32[]{:S(2)}) async-start(f32[2,64,1024]{2,0,1:T(2,128)} %reshape.469), calls=%async_computation.2 | async-start | bytes 1048576 | tf_op jit(solution)/shard_map/all_to_all | solution.py:224
  180.7 5.4 %copy.158 = f32[6,64,16,64]{3,2,1,0:T(8,128)} copy(f32[6,64,16,64]{3,1,2,0:T(8,128)} %get-tuple-element.79) | data formatting | bytes 3145728 | tf_op jit(solution)/shard_map/while | solution.py:94
  186.2 3.7 %reshape.381 = f32[1,384,1024]{2,1,0:T(8,128)} reshape(f32[6,64,16,64]{3,2,1,0:T(8,128)} %copy.158) | data formatting | bytes 3145728 | tf_op jit(solution)/shard_map/reshape | solution.py:105
  190.9 1.7 copy.160
  192.7 1.6 copy.162
  195.0 4.0 %fusion.26 = bf16[1,384,1024]{2,1,0:T(8,128)(2,1)} fusion(f32[1024]{0:T(1024)S(1)} %copy-done.25, f32[1024]{0:T(1024)S(1)} %copy-done.26, f32[1,384,1024]{2,1,0:T(8,128)} %copy.162, f32[1,384,1024]{2,1,0:T(8,128)} %reshape.381, f32[1,384,1024]{2,1,0:T(8,128)} %copy.160, pred[]{:T(512)S(1)} %bitcast.193), kind=kLoop, calls=%fused_computation.66 | loop fusion | flops 2359296 | bytes 5513217 | tf_op jit(solution)/shard_map/jit(_where)/select_n | solution.py:187
  199.2 1.5 gather_fusion.5
  (211 shorter events, 33.6 us)
Async XLA Ops:
  7.2 80.8 %copy-start = (bf16[4096,128]{1,0:T(8,128)(2,1)S(1)}, bf16[4096,128]{1,0:T(8,128)(2,1)}, u32[]{:S(2)}) copy-start(bf16[4096,128]{1,0:T(8,128)(2,1)} %param.29) | copy-start | bytes 3145732
  7.2 14.6 %copy-start.6 = (bf16[1,384,1024]{2,1,0:T(8,128)(2,1)S(1)}, bf16[1,384,1024]{2,1,0:T(8,128)(2,1)}, u32[]{:S(2)}) copy-start(bf16[1,384,1024]{2,1,0:T(8,128)(2,1)} %param.22) | copy-start | bytes 2359300
  8.0 0.5 copy-start.32
  10.5 13.6 %all-to-all-start.1 = ((bf16[8,2,128]{2,1,0:T(2,128)(2,1)}), bf16[8,2,128]{2,1,0:T(2,128)(2,1)S(1)}, u32[]{:S(2)}, u32[]{:S(2)}) async-start(bf16[8,2,128]{2,1,0:T(2,128)(2,1)} %reshape.474), calls=%async_computation.1 | async-start | bytes 8192 | tf_op jit(solution)/shard_map/all_to_all | solution.py:145
  17.8 40.0 %all-gather.5.cloned.1.call-start = ((), (), s32[]{:S(2)}) async-start(), calls=%async_computation.5 | async-start | bytes 4259840 | tf_op jit(solution)/shard_map/all_gather | solution.py:35
  17.9 6.9 %copy-start.16 = (bf16[2,16,1024]{2,1,0:T(8,128)(2,1)S(1)}, bf16[2,16,1024]{2,1,0:T(8,128)(2,1)}, u32[]{:S(2)}) copy-start(bf16[2,16,1024]{2,1,0:T(8,128)(2,1)} %param.25) | copy-start | bytes 196612
  17.9 6.9 %copy-start.23 = (f32[1024]{0:T(1024)S(1)}, f32[1024]{0:T(1024)}, u32[]{:S(2)}) copy-start(f32[1024]{0:T(1024)} %param.33) | copy-start | bytes 12292
  17.9 6.9 %copy-start.24 = (f32[1024]{0:T(1024)S(1)}, f32[1024]{0:T(1024)}, u32[]{:S(2)}) copy-start(f32[1024]{0:T(1024)} %param.34) | copy-start | bytes 12292
  20.5 7.6 %copy-start.30 = (s32[2]{0:T(128)}, s32[2]{0:T(128)S(1)}, u32[]{:S(2)}) copy-start(s32[2]{0:T(128)S(1)} %gather_fusion.4) | copy-start | bytes 28
  26.0 1.1 copy-start.19
  26.9 6.6 %copy-start.15 = (f32[16,8,1024]{2,1,0:T(8,128)S(1)}, f32[16,8,1024]{2,1,0:T(8,128)}, u32[]{:S(2)}) copy-start(f32[16,8,1024]{2,1,0:T(8,128)} %param.37) | copy-start | bytes 1572868
  27.0 61.0 %all-gather.3.cloned.1.call-start = ((), (), s32[]{:S(2)}) async-start(), calls=%async_computation.4 | async-start | bytes 4259840 | tf_op jit(solution)/shard_map/all_gather | solution.py:40
  28.0 16.2 %copy-start.20 = (f32[1024]{0:T(1024)S(1)}, f32[1024]{0:T(1024)}, u32[]{:S(2)}) copy-start(f32[1024]{0:T(1024)} %param.32) | copy-start | bytes 12292
  28.0 16.3 %copy-start.21 = (bf16[2,16,1024]{2,1,0:T(8,128)(2,1)S(1)}, bf16[2,16,1024]{2,1,0:T(8,128)(2,1)}, u32[]{:S(2)}) copy-start(bf16[2,16,1024]{2,1,0:T(8,128)(2,1)} %param.26) | copy-start | bytes 196612
  28.0 17.2 %copy-start.22 = (bf16[2,16,1024]{2,1,0:T(8,128)(2,1)S(1)}, bf16[2,16,1024]{2,1,0:T(8,128)(2,1)}, u32[]{:S(2)}) copy-start(bf16[2,16,1024]{2,1,0:T(8,128)(2,1)} %param.27) | copy-start | bytes 196612
  28.1 18.0 %copy-start.13 = (bf16[1,384,1024]{2,1,0:T(8,128)(2,1)S(1)}, bf16[1,384,1024]{2,1,0:T(8,128)(2,1)}, u32[]{:S(2)}) copy-start(bf16[1,384,1024]{2,1,0:T(8,128)(2,1)} %param.23) | copy-start | bytes 2359300
  29.9 10.1 %all-to-all-start.3 = ((bf16[8,2,128]{2,1,0:T(2,128)(2,1)}), bf16[8,2,128]{2,1,0:T(2,128)(2,1)S(1)}, u32[]{:S(2)}, u32[]{:S(2)}) async-start(bf16[8,2,128]{2,1,0:T(2,128)(2,1)} %reshape.476), calls=%async_computation.3 | async-start | bytes 8192 | tf_op jit(solution)/shard_map/all_to_all | solution.py:225
  40.0 16.3 %all-to-all-start = ((f32[16,8,1024]{2,1,0:T(8,128)}), f32[16,8,1024]{2,1,0:T(8,128)S(1)}, u32[]{:S(2)}, u32[]{:S(2)}) async-start(f32[16,8,1024]{2,1,0:T(8,128)} %gather_fusion.2), calls=%async_computation | async-start | bytes 1048576 | tf_op jit(solution)/shard_map/all_to_all | solution.py:144
  46.0 2.2 %copy-start.14 = (bf16[1,384,1024]{2,1,0:T(8,128)(2,1)S(1)}, bf16[1,384,1024]{2,1,0:T(8,128)(2,1)}, u32[]{:S(2)}) copy-start(bf16[1,384,1024]{2,1,0:T(8,128)(2,1)} %param.24) | copy-start | bytes 2359300
  48.2 2.7 %copy-start.31 = (s32[2]{0:T(128)S(1)}, s32[2]{0:T(128)}, u32[]{:S(2)}) copy-start(s32[2]{0:T(128)} %copy-done.30) | copy-start | bytes 28
  50.9 6.6 %copy-start.28 = (s32[1024]{0:T(1024)}, s32[1024]{0:T(1024)S(1)}, u32[]{:S(2)}) copy-start(s32[1024]{0:T(1024)S(1)} %pad_clamp_fusion) | copy-start | bytes 12292
  56.6 1.0 copy-start.3
  65.9 22.1 %copy-start.17 = (bf16[128,1024]{1,0:T(8,128)(2,1)S(1)}, bf16[128,1024]{1,0:T(8,128)(2,1)}, u32[]{:S(2)}) copy-start(bf16[128,1024]{1,0:T(8,128)(2,1)} %param.30) | copy-start | bytes 786436
  91.7 1.2 copy-start.5
  91.7 1.2 copy-start.18
  91.7 2.8 %copy-start.29 = (pred[2,16]{1,0:T(4,128)(4,1)S(1)}, pred[2,16]{1,0:T(4,128)(4,1)}, u32[]{:S(2)}) copy-start(pred[2,16]{1,0:T(4,128)(4,1)} %iota_compare_fusion.2) | copy-start | bytes 100
  91.7 2.9 %copy-start.10 = (f32[2,16,16,64]{3,2,1,0:T(8,128)S(1)}, f32[2,16,16,64]{3,2,1,0:T(8,128)}, u32[]{:S(2)}) copy-start(f32[2,16,16,64]{3,2,1,0:T(8,128)} %reshape.387) | copy-start | bytes 393220
  91.7 2.9 %copy-start.11 = (f32[2,16,16,64]{3,2,1,0:T(8,128)S(1)}, f32[2,16,16,64]{3,2,1,0:T(8,128)}, u32[]{:S(2)}) copy-start(f32[2,16,16,64]{3,2,1,0:T(8,128)} %reshape.388) | copy-start | bytes 393220
  93.0 2.9 %slice-start = ((f32[416,1024]{1,0:T(8,128)}), f32[384,1024]{1,0:T(8,128)S(1)}, s32[]{:S(2)}) async-start(f32[416,1024]{1,0:T(8,128)} %copy-done.5), calls=%async_computation.6 | async-start | bytes 3145728 | tf_op jit(solution)/shard_map/slice | solution.py:182
  106.3 2.1 %copy-start.2 = (f32[64,16,64]{2,1,0:T(8,128)S(1)}, f32[64,16,64]{2,1,0:T(8,128)}, u32[]{:S(2)}) copy-start(f32[64,16,64]{2,1,0:T(8,128)} %get-tuple-element.244) | copy-start | bytes 786436 | tf_op jit(solution)/shard_map/while
  116.4 2.1 %copy-start.2 = (f32[64,16,64]{2,1,0:T(8,128)S(1)}, f32[64,16,64]{2,1,0:T(8,128)}, u32[]{:S(2)}) copy-start(f32[64,16,64]{2,1,0:T(8,128)} %get-tuple-element.244) | copy-start | bytes 786436 | tf_op jit(solution)/shard_map/while
  126.5 2.1 %copy-start.2 = (f32[64,16,64]{2,1,0:T(8,128)S(1)}, f32[64,16,64]{2,1,0:T(8,128)}, u32[]{:S(2)}) copy-start(f32[64,16,64]{2,1,0:T(8,128)} %get-tuple-element.244) | copy-start | bytes 786436 | tf_op jit(solution)/shard_map/while
  136.5 2.1 %copy-start.2 = (f32[64,16,64]{2,1,0:T(8,128)S(1)}, f32[64,16,64]{2,1,0:T(8,128)}, u32[]{:S(2)}) copy-start(f32[64,16,64]{2,1,0:T(8,128)} %get-tuple-element.244) | copy-start | bytes 786436 | tf_op jit(solution)/shard_map/while
  146.6 2.1 %copy-start.2 = (f32[64,16,64]{2,1,0:T(8,128)S(1)}, f32[64,16,64]{2,1,0:T(8,128)}, u32[]{:S(2)}) copy-start(f32[64,16,64]{2,1,0:T(8,128)} %get-tuple-element.244) | copy-start | bytes 786436 | tf_op jit(solution)/shard_map/while
  156.6 2.1 %copy-start.2 = (f32[64,16,64]{2,1,0:T(8,128)S(1)}, f32[64,16,64]{2,1,0:T(8,128)}, u32[]{:S(2)}) copy-start(f32[64,16,64]{2,1,0:T(8,128)} %get-tuple-element.244) | copy-start | bytes 786436 | tf_op jit(solution)/shard_map/while
  164.6 3.7 %copy-start.4 = (f32[2,64,16,64]{3,2,1,0:T(8,128)S(1)}, f32[2,64,16,64]{3,2,1,0:T(8,128)}, u32[]{:S(2)}) copy-start(f32[2,64,16,64]{3,2,1,0:T(8,128)} %copy-done.3) | copy-start | bytes 1572868
  167.9 1.0 copy-start.12
  168.3 2.0 copy-start.8
  168.3 2.0 copy-start.9
  168.3 2.0 copy-start.27
  168.5 2.9 %copy-start.7 = (f32[2,16,16,64]{3,2,1,0:T(8,128)S(1)}, f32[2,16,16,64]{3,2,1,0:T(8,128)}, u32[]{:S(2)}) copy-start(f32[2,16,16,64]{3,2,1,0:T(8,128)} %get-tuple-element.172) | copy-start | bytes 393220
  174.7 24.3 %all-to-all-start.2 = ((f32[2,64,1024]{2,0,1:T(2,128)}), f32[2,64,1024]{2,0,1:T(2,128)S(1)}, u32[]{:S(2)}, u32[]{:S(2)}) async-start(f32[2,64,1024]{2,0,1:T(2,128)} %reshape.469), calls=%async_computation.2 | async-start | bytes 1048576 | tf_op jit(solution)/shard_map/all_to_all | solution.py:224
  192.7 1.6 copy-start.25
  192.7 1.6 copy-start.26
  195.0 5.7 %copy-start.1 = (bf16[4096,128]{1,0:T(8,128)(2,1)S(1)}, bf16[4096,128]{1,0:T(8,128)(2,1)}, u32[]{:S(2)}) copy-start(bf16[4096,128]{1,0:T(8,128)(2,1)} %param.29) | copy-start | bytes 3145732
Sparse Core Ops, SparseCore 0:
  27.1 29.1 all-gather.4
  57.9 30.0 all-gather.2
where the time goes:
time: 209 us; the launch traced here: 208 us
  local copies, waits for them, and re-layouts  52.7 us (25%)
  matrix products  46.4 us (22%)
  other arithmetic  42.3 us (20%)
  waiting for transfers between devices  30.8 us (15%)
  starting transfers between devices  20.2 us (10%)
  between operations  14.7 us (7%)
    all_gather x1, waiting for transfers between devices, project(): lax.all_gather(decay_mixed_input, 'tp', axis=1, tiled=True)  20.1 us
    mul x6, other arithmetic, one_block(): keys_scaled = address_vectors_all * jnp.exp(middle - inclusive)  15 us
    dot_general x7, matrix products, one_block(): jnp.einsum('thi,hij->thj', accept_vectors_all * jnp.exp(exclusive), threa...  12 us
    dot_general x7, matrix products, one_block(): jnp.einsum('thi,shi->hts', recept_scaled, keys_scaled, precision=HIGH)  8.27 us
    dot_general x1, matrix products, project(): jnp.dot(lax.all_gather(mixed_value, 'tp', axis=1, tiled=True), content_ma...  8.09 us
    another operation x7, other arithmetic, one_block(): inclusive = jnp.cumsum(rate_b, axis=0)  8.08 us
    dot_general x6, matrix products, one_block(): jnp.einsum('shi,shj->hij', address_vectors_all * jnp.exp(total - inclusiv...  7.83 us
    all_to_all x1, starting transfers between devices, local(): lax.all_to_all(ordered_shift, 'rep', split_axis=0, concat_axis=1, tiled=T...  7.25 us
  transfers between devices with their start and end apart: 6, of which 4 were waited for; matrix products, arithmetic and copies ran while one was open for 22% of the time, Pallas kernels for 0%

commit v1 on v0

v1 whole, which is shorter than its diff:
```python
import functools

import jax
import jax.numpy as jnp
from jax import lax
from jax.experimental import pallas as pl
from jax.experimental.pallas import tpu as pltpu
from jax.sharding import PartitionSpec as P

SPAN = 64
DRAFT = 16
PAIR = 2 * SPAN
CHUNK = 64
PIECES = 3
EXTRA = 16
TAIL_FIRST, TAIL_LAST, MIX_V, MIX_W = 0, 1, 2, 5
EPS = 0.00064
SAFE = -60.0
F32, BF16 = jnp.float32, jnp.bfloat16
VMEM_BYTES = 40 * 1024 * 1024
VMEM = pl.BlockSpec(memory_space=pltpu.VMEM)
SMEM = pl.BlockSpec(memory_space=pltpu.SMEM)
ANYWHERE = pl.BlockSpec(memory_space=pl.ANY)


def params():
    return pltpu.CompilerParams(vmem_limit_bytes=VMEM_BYTES)


def iota(shape, dim):
    return lax.broadcasted_iota(jnp.int32, shape, dim)


def split2(x):
    high = x.astype(BF16)
    return high, (x - high.astype(F32)).astype(BF16)


def split3(x):
    high = x.astype(BF16)
    rest = x - high.astype(F32)
    mid = rest.astype(BF16)
    return high, mid, (rest - mid.astype(F32)).astype(BF16)


def dot(a, b):
    return jnp.dot(a, b, preferred_element_type=F32)


def dot_rows(a, b):
    return lax.dot_general(a, b, (((0,), (0,)), ((), ())), preferred_element_type=F32)


def dot_lanes(a, b):
    return lax.dot_general(a, b, (((1,), (1,)), ((), ())), preferred_element_type=F32)


def pack_kernel(
    slots,
    owner,
    state,
    prior,
    draft,
    head,
    foot,
    mix_v,
    mix_w,
    state_out,
    prior_out,
    small_out,
):
    groups = state_out.shape[0]
    copies = prior_out.shape[0] // groups
    heads = prior.shape[2]
    place_row, place_lane = iota((heads, 128), 0), iota((heads, 128), 1)
    for g in range(groups):
        reqs = [owner[g * slots + s] for s in range(slots)]
        rows = jnp.concatenate([state[q] for q in reqs], axis=0)
        state_out[g] = rows.astype(BF16)
        spread = sum(
            dot(prior[q], (place_lane == place_row + s * heads).astype(BF16))
            for s, q in enumerate(reqs)
        )
        for c in range(copies):
            prior_out[g * copies + c] = spread
    for s in range(slots):
        small_out[s * DRAFT : (s + 1) * DRAFT, :] = draft[s]
    width = small_out.shape[1]
    row = iota((EXTRA, width), 0)
    rest = jnp.where(row == TAIL_FIRST, head[...].astype(F32)[0:1], 0.0)
    rest = jnp.where(row == TAIL_LAST, foot[...].astype(F32)[EXTRA - 1 : EXTRA], rest)
    for base, share in ((MIX_V, mix_v), (MIX_W, mix_w)):
        for n, part in enumerate(split3(share[...])):
            rest = jnp.where(row == base + n, part.astype(F32), rest)
    small_out[slots * DRAFT :, :] = rest.astype(BF16)


def pack(lane_owner, state, prior, draft, tail, mix_v, mix_w, groups, copies):
    reqs, lines, width = state.shape
    slots = draft.shape[0]
    last = tail.shape[0] // EXTRA - 1
    whole = lambda *shape: pl.BlockSpec(shape, lambda i: (0,) * len(shape))
    return pl.pallas_call(
        functools.partial(pack_kernel, slots),
        grid=(1,),
        in_specs=[
            SMEM,
            whole(*state.shape),
            whole(*prior.shape),
            whole(*draft.shape),
            pl.BlockSpec((EXTRA, width), lambda i: (0, 0)),
            pl.BlockSpec((EXTRA, width), lambda i: (last, 0)),
            whole(1, width),
            whole(1, width),
        ],
        out_specs=[
            whole(groups, slots * lines, width),
            whole(groups * copies, lines, 128),
            whole(slots * DRAFT + EXTRA, width),
        ],
        out_shape=[
            jax.ShapeDtypeStruct((groups, slots * lines, width), BF16),
            jax.ShapeDtypeStruct((groups * copies, lines, 128), F32),
            jax.ShapeDtypeStruct((slots * DRAFT + EXTRA, width), BF16),
        ],
        compiler_params=params(),
        name="pack",
    )(lane_owner, state, prior, draft, tail, tail, mix_v, mix_w)


def prior_row(prior, block, copies, slot, heads, width):
    groups = prior.shape[0] // copies
    lines = jnp.concatenate([prior[g * copies + block] for g in range(groups)], axis=0)
    lane = iota((128, width), 1)
    place = (iota((128, width), 0) == slot * heads + lane // SPAN).astype(BF16)
    spread = dot(lines.astype(BF16), place)
    keep = iota((SPAN, width), 0) == iota((SPAN, width), 1) % SPAN
    return jnp.sum(jnp.where(keep, spread, 0.0), axis=0, keepdims=True)


def mixed(x, previous, share):
    return (x + (previous - x) * share).astype(BF16)


def project_kernel(slots, copies, has_before, has_draft, *refs):
    refs = list(refs)
    take = lambda n: [refs.pop(0) for _ in range(n)]
    owner, spans = take(2)
    xs = take(copies)
    before = take(copies) if has_before else None
    smalls = take(copies)
    shrink, expand, anchor, weights = take(4)
    prior = take(1)[0] if has_draft else None
    v_out, w_out = take(2)
    vd_out, wd_out = take(2) if has_draft else (None, None)
    acc_v, acc_w, held, sems = take(4)
    width = v_out.shape[1]
    rows = v_out.shape[0]
    drafts = slots * DRAFT
    me = lax.axis_index("tp")
    blocks = [jnp.bitwise_xor(me, j) for j in range(copies)]

    def fetch(j):
        start = pl.multiple_of(blocks[j] * width, width)
        return pltpu.make_async_copy(weights.at[pl.ds(start, width), :], held.at[j], sems.at[j])

    for j in range(copies):
        fetch(j).start()
    if has_draft:
        first_slot = lax.axis_index("rep") * slots
        is_long = [spans[owner[first_slot + s]] > DRAFT for s in range(slots)]
    for j in range(copies):
        x = xs[j][...].astype(F32)
        row = iota(x.shape, 0)
        previous = pltpu.roll(x, 1, 0)
        if has_before:
            previous = jnp.where(row == 0, before[j][...].astype(F32)[EXTRA - 1 : EXTRA], previous)
        rest = smalls[j][drafts:, :].astype(F32)
        share_v = rest[MIX_V : MIX_V + 1] + rest[MIX_V + 1 : MIX_V + 2] + rest[MIX_V + 2 : MIX_V + 3]
        share_w = rest[MIX_W : MIX_W + 1] + rest[MIX_W + 1 : MIX_W + 2] + rest[MIX_W + 2 : MIX_W + 3]
        xv, xw = mixed(x, previous, share_v), mixed(x, previous, share_w)
        if has_draft:
            d = smalls[j][...].astype(F32)
            row = iota(d.shape, 0)
            previous = pltpu.roll(d, 1, 0)
            for s in range(slots):
                prior_first = prior_row(prior, blocks[j], copies, s, width // SPAN, width)
                first = jnp.where(is_long[s], rest[TAIL_LAST : TAIL_LAST + 1], prior_first)
                previous = jnp.where(row == s * DRAFT, first, previous)
                if s == 0:
                    previous = jnp.where(row == drafts + TAIL_FIRST, prior_first, previous)
            xv = jnp.concatenate([xv, mixed(d, previous, share_v)], axis=0)
            xw = jnp.concatenate([xw, mixed(d, previous, share_w)], axis=0)
        low = dot(xw, shrink[pl.ds(pl.multiple_of(blocks[j] * width, width), width), :])
        fetch(j).wait()
        part = dot(xv, held[j])
        if j == 0:
            acc_w[...] = low
            acc_v[...] = part
        else:
            acc_w[...] += low
            acc_v[...] += part
    rate = -jnp.exp(anchor[...] + dot(jnp.tanh(acc_w[...]).astype(BF16), expand[...]))
    v_out[...] = acc_v[0:rows, :].astype(BF16)
    w_out[...] = rate[0:rows]
    if has_draft:
        vd_out[...] = acc_v[rows:, :].astype(BF16)
        wd_out[...] = rate[rows:]


def project(
    piece,
    lane_owner,
    spans,
    wholes,
    parts,
    befores,
    smalls,
    shrink,
    expand,
    anchor,
    weights,
    prior,
    slots,
    rows,
):
    copies = len(smalls)
    width = weights.shape[1]
    drafts = smalls[0].shape[0]
    whole = lambda shape: pl.BlockSpec(shape, lambda i: (0,) * len(shape))
    has_before, has_draft = piece > 0, prior is not None
    per = rows // EXTRA
    in_specs = [SMEM, SMEM]
    in_specs += [pl.BlockSpec((rows, width), lambda i: (piece, 0)) for _ in wholes]
    in_specs += [whole((rows, width)) for _ in parts]
    args = [lane_owner, spans, *wholes, *parts]
    if has_before:
        in_specs += [pl.BlockSpec((EXTRA, width), lambda i: (piece * per - 1, 0)) for _ in wholes]
        in_specs += [pl.BlockSpec((EXTRA, width), lambda i: (per - 1, 0)) for _ in befores]
        args += [*wholes, *befores]
    for array in (*smalls, shrink, expand, anchor):
        in_specs.append(whole(array.shape))
        args.append(array)
    in_specs.append(ANYWHERE)
    args.append(weights)
    outs = [((rows, width), BF16), ((rows, width), F32)]
    total = rows
    if has_draft:
        in_specs.append(whole(prior.shape))
        args.append(prior)
        outs += [((drafts, width), BF16), ((drafts, width), F32)]
        total += drafts
    return pl.pallas_call(
        functools.partial(project_kernel, slots, copies, has_before, has_draft),
        grid=(1,),
        in_specs=in_specs,
        out_specs=[whole(s) for s, _ in outs],
        out_shape=[jax.ShapeDtypeStruct(s, t) for s, t in outs],
        scratch_shapes=[
            pltpu.VMEM((total, width), F32),
            pltpu.VMEM((total, shrink.shape[1]), F32),
            pltpu.VMEM((copies, width, width), BF16),
            pltpu.SemaphoreType.DMA((copies,)),
        ],
        compiler_params=params(),
        cost_estimate=pl.CostEstimate(
            flops=2 * total * weights.shape[0] * width,
            bytes_accessed=2 * weights.shape[0] * width,
            transcendentals=0,
        ),
        name=f"project_{piece}",
    )(*args)


def lane_low(shape):
    return iota(shape, 1) < SPAN


def by_head(x):
    low = lane_low(x.shape)
    return jnp.concatenate([jnp.where(low, x, 0.0), jnp.where(low, 0.0, x)], axis=0)


def head_sum(x):
    high, low = split2(x)
    r, c = iota((2 * PAIR, PAIR), 0), iota((2 * PAIR, PAIR), 1)
    same = ((r // SPAN) % 2 == c // SPAN).astype(BF16)
    return dot(jnp.concatenate([high, low], axis=1), same)


def down(line):
    return jnp.transpose(jnp.broadcast_to(line, (PAIR, PAIR)))


def per_segment(lines, length):
    if len(lines) == 1:
        return lines[0]
    return jnp.concatenate([jnp.broadcast_to(x, (length, x.shape[1])) for x in lines], axis=0)


def running(rate, length):
    n = rate.shape[0]
    t, s = iota((n, 3 * n), 0), iota((n, 3 * n), 1) % n
    upto = ((s <= t) & (s // length == t // length)).astype(BF16)
    return dot(upto, jnp.concatenate(split3(rate), axis=0))


def scores_scaled(r, k, rate, inclusive, middle, length):
    n = r.shape[0]
    rt = r * jnp.exp(inclusive - rate - middle)
    kt = k * jnp.exp(middle - inclusive)
    sc = dot_lanes(by_head(rt).astype(BF16), kt.astype(BF16))
    t, s = iota((2 * n, n), 0) % n, iota((2 * n, n), 1)
    return jnp.where((s < t) & (s // length == t // length), sc, 0.0)


def scores_levels(r, k, rate, length):
    n = r.shape[0]
    pieces = split3(rate)
    levels = length.bit_length() - 1

    def level(n_level, total):
        half = lax.shift_left(jnp.int32(1), n_level)
        shift = n_level + 1
        t, u = iota((n, 3 * n), 0), iota((n, 3 * n), 1) % n
        edge = lax.shift_left(lax.shift_right_logical(t, shift), shift) + half
        after = (t >= edge) & (u >= edge) & (u < t)
        ahead = (t < edge) & (u > t) & (u < edge)
        decay = jnp.exp(dot((after | ahead).astype(BF16), jnp.concatenate(pieces, axis=0)))
        row = iota(r.shape, 0)
        row_edge = lax.shift_left(lax.shift_right_logical(row, shift), shift) + half
        rt = jnp.where(row >= row_edge, r * decay, 0.0)
        kt = jnp.where(row < row_edge, k * decay, 0.0)
        sc = dot_lanes(by_head(rt).astype(BF16), kt.astype(BF16))
        t2, s2 = iota((2 * n, n), 0) % n, iota((2 * n, n), 1)
        same = lax.shift_right_logical(t2, shift) == lax.shift_right_logical(s2, shift)
        return total + jnp.where(same, sc, 0.0)

    return lax.fori_loop(0, levels, level, jnp.zeros((2 * n, n), F32))


def answers(r, k, v, rate, boost, states, length, scaled):
    n = r.shape[0]
    count = n // length
    inclusive = running(rate, length)
    if scaled:
        middle = per_segment(
            [inclusive[s * length + length // 2 : s * length + length // 2 + 1] for s in range(count)],
            length,
        )
        sc = scores_scaled(r, k, rate, inclusive, middle, length)
    else:
        sc = scores_levels(r, k, rate, length)
    inner = dot(sc.astype(BF16), v)
    y = jnp.where(lane_low((n, PAIR)), inner[:n], inner[n:])
    rs = (r * jnp.exp(inclusive - rate)).astype(BF16)
    outer = [dot(rs[s * length : (s + 1) * length], states[s].astype(BF16)) for s in range(count)]
    y = y + (outer[0] if count == 1 else jnp.concatenate(outer, axis=0))
    y = y + head_sum(r * k * boost) * v.astype(F32)
    return y, inclusive


def gathered(keys, v):
    high, low = split2(keys)
    full = dot_rows(jnp.concatenate([high, low], axis=0), jnp.concatenate([v, v], axis=0))
    same = (iota((PAIR, PAIR), 0) < SPAN) == (iota((PAIR, PAIR), 1) < SPAN)
    return jnp.where(same, full, 0.0)


def normed(y, gain, bias):
    center = y - head_sum(y) * (1.0 / SPAN)
    spread = head_sum(center * center) * (1.0 / SPAN)
    return (center * lax.rsqrt(spread + EPS) * gain + bias).astype(BF16)


def mix_kernel(slots, copies, direct, *refs):
    refs = list(refs)
    take = lambda n: [refs.pop(0) for _ in range(n)]
    owner, spans, admitted = take(3)
    vs, ws = take(PIECES), take(PIECES)
    v_draft, w_draft, r_tail, k_tail, r_draft, k_draft, got, small, prior = take(9)
    boost, gain, bias = take(3)
    tail_out, draft_out, back = take(3)
    v_all, w_all, states = take(3)
    width = v_all.shape[1]
    pairs = width // PAIR
    rows = vs[0].shape[0]
    total = rows * PIECES
    drafts = slots * DRAFT
    first_slot = lax.axis_index("rep") * slots
    reqs = [owner[first_slot + s] for s in range(slots)]
    is_long = [spans[q] > DRAFT for q in reqs]
    me = lax.axis_index("tp")

    groups = got.shape[0]
    lines = SPAN // groups
    for s in range(slots):
        begin = jnp.concatenate(
            [got[g].astype(F32)[s * lines : (s + 1) * lines] for g in range(groups)], axis=0
        )
        for p in range(pairs):
            b = begin[:, p * PAIR : (p + 1) * PAIR]
            low = lane_low(b.shape)
            states[s, p] = jnp.concatenate([jnp.where(low, b, 0.0), jnp.where(low, 0.0, b)], axis=0)

    def chunk_pair(c, p, scaled):
        at = pl.ds(pl.multiple_of(c * CHUNK, CHUNK), CHUNK)
        lanes = pl.ds(p * PAIR if isinstance(p, int) else pl.multiple_of(p * PAIR, PAIR), PAIR)
        r, k = r_tail[at, lanes].astype(F32), k_tail[at, lanes].astype(F32)
        v, rate = v_all[at, lanes], w_all[at, lanes]
        state = states[0, p]
        y, inclusive = answers(r, k, v, rate, boost[:, lanes], [state], CHUNK, scaled)
        closing = inclusive[CHUNK - 1 : CHUNK]
        states[0, p] = down(jnp.exp(closing)) * state + gathered(k * jnp.exp(closing - inclusive), v)
        tail_out[at, lanes] = normed(y, gain[:, lanes], bias[:, lanes])

    @pl.when(is_long[0])
    def _():
        lowest = jnp.zeros((1, width), F32)
        for n in range(PIECES):
            v, w = vs[n][...], ws[n][...]
            if n == 0:
                row = iota(w.shape, 0)
                start = drafts + TAIL_FIRST
                w = jnp.where(row == 0, w_draft[...][start : start + 1], w)
                v = jnp.where(row == 0, v_draft[...].astype(F32)[start : start + 1], v.astype(F32)).astype(BF16)
            v_all[n * rows : (n + 1) * rows, :] = v
            w_all[n * rows : (n + 1) * rows, :] = w
            for c in range(rows // CHUNK):
                lowest = jnp.minimum(
                    lowest, jnp.sum(w[c * CHUNK : (c + 1) * CHUNK], axis=0, keepdims=True)
                )
        safe = jnp.min(lowest) > SAFE

        @pl.when(safe)
        def _():
            def body(c, carry):
                for p in range(pairs):
                    chunk_pair(c, p, True)
                return carry

            lax.fori_loop(0, total // CHUNK, body, 0)

        @pl.when(jnp.logical_not(safe))
        def _():
            def body(n, carry):
                chunk_pair(n // pairs, n % pairs, False)
                return carry

            lax.fori_loop(0, total // CHUNK * pairs, body, 0)

    @pl.when(jnp.logical_not(is_long[0]))
    def _():
        tail_out[...] = jnp.zeros_like(tail_out)

    counts = [admitted[q] for q in reqs]
    lowest = jnp.min(
        jnp.concatenate(
            [
                jnp.sum(w_draft[s * DRAFT : (s + 1) * DRAFT, :], axis=0, keepdims=True)
                for s in range(slots)
            ],
            axis=0,
        )
    )
    safe = lowest > SAFE

    def draft_pair(p, scaled):
        lanes = pl.ds(p * PAIR if isinstance(p, int) else pl.multiple_of(p * PAIR, PAIR), PAIR)
        r, k = r_draft[:, lanes].astype(F32), k_draft[:, lanes].astype(F32)
        v, rate = v_draft[0:drafts, lanes], w_draft[0:drafts, lanes]
        begin = [states[s, p] for s in range(slots)]
        y, inclusive = answers(r, k, v, rate, boost[:, lanes], begin, DRAFT, scaled)
        draft_out[:, lanes] = normed(y, gain[:, lanes], bias[:, lanes])
        row = iota((drafts, PAIR), 0)
        ends = []
        for s in range(slots):
            taken = (row >= s * DRAFT) & (row < s * DRAFT + counts[s])
            upto = jnp.sum(jnp.where(taken, rate, 0.0), axis=0, keepdims=True)
            weight = jnp.where(taken, jnp.exp(jnp.minimum(upto - inclusive, 0.0)), 0.0)
            end = down(jnp.exp(upto)) * begin[s] + gathered(k * weight, v)
            ends.append(end[:SPAN] + end[SPAN:])
        if direct:
            for g in range(groups):
                part = jnp.concatenate([e[g * lines : (g + 1) * lines] for e in ends], axis=0)
                back[g, :, lanes] = part.astype(BF16)
        else:
            for s in range(slots):
                back[s, :, lanes] = ends[s].astype(BF16)

    @pl.when(safe)
    def _():
        for p in range(pairs):
            draft_pair(p, True)

    @pl.when(jnp.logical_not(safe))
    def _():
        def body(p, carry):
            draft_pair(p, False)
            return carry

        lax.fori_loop(0, pairs, body, 0)

    heads = width // SPAN
    tokens = small[...].astype(F32)
    row = iota((drafts + EXTRA, width), 0)
    place = (iota((128, width), 0) == iota((128, width), 1) // SPAN).astype(BF16)
    keep = iota((SPAN, width), 0) == iota((SPAN, width), 1) % SPAN
    edges = []
    for s in range(slots):
        own = prior_row(prior, me, copies, s, heads, width)
        last = drafts + TAIL_LAST
        first = jnp.where(is_long[s], tokens[last : last + 1], own)
        chosen = jnp.sum(jnp.where(row == s * DRAFT + counts[s] - 1, tokens, 0.0), axis=0, keepdims=True)
        edge = jnp.where(counts[s] > 0, chosen, first)
        edges.append(dot_lanes(jnp.where(keep, edge, 0.0).astype(BF16), place))
    if direct:
        for g in range(groups):
            part = jnp.concatenate([e[g * lines : (g + 1) * lines] for e in edges], axis=0)
            back[g, :, width:] = part.astype(BF16)
    else:
        for s in range(slots):
            back[s, :, width:] = edges[s].astype(BF16)


def time_mix(scalars, vs, ws, arrays, slots, copies):
    width = vs[0].shape[1]
    rows = vs[0].shape[0]
    got = arrays[6]
    groups = got.shape[0]
    direct = SPAN // groups == 8
    back = (groups, slots * SPAN // groups) if direct else (slots, SPAN)
    back = (*back, width + 128)
    outs = [((rows * PIECES, width), BF16), ((slots * DRAFT, width), BF16), (back, BF16)]
    tail_out, draft_out, ret = pl.pallas_call(
        functools.partial(mix_kernel, slots, copies, direct),
        in_specs=[SMEM] * len(scalars) + [VMEM] * (2 * PIECES + len(arrays)),
        out_specs=[VMEM] * 3,
        out_shape=[jax.ShapeDtypeStruct(s, t) for s, t in outs],
        scratch_shapes=[
            pltpu.VMEM((rows * PIECES, width), BF16),
            pltpu.VMEM((rows * PIECES, width), F32),
            pltpu.VMEM((slots, width // PAIR, PAIR, PAIR), F32),
        ],
        compiler_params=params(),
        name="time_mix",
    )(*scalars, *vs, *ws, *arrays)
    if not direct:
        lines = SPAN // groups
        ret = ret.reshape(slots, groups, lines, width + 128).transpose(1, 0, 2, 3)
        ret = ret.reshape(groups, slots * lines, width + 128)
    return tail_out, draft_out, ret


def unpack_kernel(slots, owner, back, state_out, shift_out):
    reqs, lines, width = state_out.shape
    heads = shift_out.shape[2]
    for g in range(reqs // slots):
        rows = back[g].astype(F32)
        for s in range(slots):
            q = owner[g * slots + s]
            mine = rows[s * lines : (s + 1) * lines]
            state_out[q] = mine[:, :width]
            shift_out[q] = mine[:, width : width + heads].astype(BF16)


def unpack(lane_owner, back, slots, lines, width, heads):
    reqs = back.shape[0] * slots
    return pl.pallas_call(
        functools.partial(unpack_kernel, slots),
        in_specs=[SMEM, VMEM],
        out_specs=[VMEM, VMEM],
        out_shape=[
            jax.ShapeDtypeStruct((reqs, lines, width), F32),
            jax.ShapeDtypeStruct((reqs, lines, heads), BF16),
        ],
        compiler_params=params(),
        name="unpack",
    )(lane_owner, back)


def local(
    groups,
    copies,
    suffix_source,
    suffix_accept,
    suffix_address,
    guess_lane_source,
    guess_lane_accept,
    guess_lane_address,
    content_map,
    forget_shrink_map,
    forget_expand_map,
    forget_lane_anchor,
    present_boost,
    content_blend_share,
    forget_blend_share,
    lane_normal_scale,
    lane_normal_shift,
    kernel_memory_saved,
    prior_source_saved,
    lane_owner,
    request_spans,
    admitted_guesses,
):
    width = content_map.shape[1]
    slots = guess_lane_source.shape[0]
    drafts = slots * DRAFT
    lines = kernel_memory_saved.shape[1]
    line = lambda x: x.reshape(1, width)

    def flip(x, k):
        return lax.ppermute(x, "tp", [(i, i ^ k) for i in range(copies)])

    tail = suffix_source[0]
    rows = tail.shape[0] // PIECES
    state_sent, prior_sent, small = pack(
        lane_owner,
        kernel_memory_saved,
        prior_source_saved,
        guess_lane_source,
        tail,
        line(content_blend_share),
        line(forget_blend_share),
        groups,
        copies,
    )
    cross = [flip(tail[n * rows : (n + 1) * rows], 2) for n in range(PIECES)]
    near = flip(tail, 1)
    smalls = [small] + [flip(small, k) for k in range(1, copies)]
    got = lax.all_to_all(state_sent, "rep", 0, 0)
    prior = lax.all_to_all(prior_sent, ("rep", "tp"), 0, 0)
    far = [flip(x, 1) for x in cross]
    vs, ws = [], []
    for n in range(PIECES):
        out = project(
            n,
            lane_owner,
            request_spans,
            [tail, near],
            [cross[n], far[n]],
            [cross[n - 1], far[n - 1]] if n else [],
            smalls,
            forget_shrink_map,
            forget_expand_map,
            line(forget_lane_anchor),
            content_map,
            prior if n == PIECES - 1 else None,
            slots,
            rows,
        )
        vs.append(out[0])
        ws.append(out[1])
    v_draft, w_draft = out[2:]
    tail_out, draft_out, ret = time_mix(
        (lane_owner, request_spans, admitted_guesses),
        vs,
        ws,
        (
            v_draft,
            w_draft,
            suffix_accept[0],
            suffix_address[0],
            guess_lane_accept.reshape(drafts, width),
            guess_lane_address.reshape(drafts, width),
            got,
            small,
            prior,
            line(present_boost),
            line(lane_normal_scale),
            line(lane_normal_shift),
        ),
        slots,
        copies,
    )
    back = lax.all_to_all(ret, "rep", 0, 0)
    state_out, shift_out = unpack(lane_owner, back, slots, lines, width, width // SPAN)
    return (
        tail_out[None],
        draft_out.reshape(slots, DRAFT, width),
        state_out,
        shift_out,
    )


def solution(mesh):
    wide = P("rep", None, "tp")
    cached = P(None, "rep", "tp")
    placed = (wide,) * 6 + (P(None, "tp"), P(), P(None, "tp")) + (P("tp"),) * 6
    placed += (cached, cached, P(), P(), P())
    return jax.shard_map(
        functools.partial(local, mesh.shape["rep"], mesh.shape["tp"]),
        mesh=mesh,
        in_specs=placed,
        out_specs=(wide, wide, cached, cached),
        check_vma=False,
    )
```

time: 209 us -> 129 us (0.62)
  matrix products: 46.4 us -> 0 us
  other arithmetic: 42.3 us -> 0.01 us
  blocking collectives: 0 us -> 38.2 us
  Pallas kernels: 0 us -> 21.7 us
  waiting for transfers between devices: 30.8 us -> 10 us
  local copies, waits for them, and re-layouts: 52.7 us -> 37.8 us
  between operations: 14.7 us -> 0.87 us
    dot_general x30 -> x0, matrix products: 46.4 us -> none  [the longest x7 12 us: one_block(): jnp.einsum('thi,hij->thj', accept_vectors_all * jnp.exp(exclusive), threa...]
    all_to_all x0 -> x1, blocking collectives: none -> 38.2 us  [local(): back = lax.all_to_all(ret, 'rep', 0, 0)]
    unnamed x69 -> x98, local copies, waits for them, and re-layouts: 4.87 us -> 36.7 us
    pallas_call x0 -> x6, Pallas kernels: none -> 21.7 us  [the longest x3 12.8 us: project(): pl.pallas_call(functools.partial(project_kernel, slots, copies, has_befor...]
    all_gather x2 -> x0, waiting for transfers between devices: 20.1 us -> none  [the longest x1 20.1 us: project(): lax.all_gather(decay_mixed_input, 'tp', axis=1, tiled=True)]
    mul x7 -> x0, other arithmetic: 16.2 us -> none  [the longest x6 15 us: one_block(): keys_scaled = address_vectors_all * jnp.exp(middle - inclusive)]
    all_to_all x4 -> x2, waiting for transfers between devices: 10.7 us -> 0.01 us  [the longest x1 0.01 us: local(): prior = lax.all_to_all(prior_sent, ('rep', 'tp'), 0, 0)]
    gather x10 -> x0, local copies, waits for them, and re-layouts: 10.1 us -> none  [the longest x1 1.5 us: local(): state_out = back_state[inverse]]
  transfers between devices with their start and end apart: 6 -> 12, of which waited for: 4 -> 2; matrix products, arithmetic and copies ran while one was open for 22% -> 1% of each run, Pallas kernels for 0% -> 11%
where the time goes in v1:
time: 129 us; the launch traced here: 127 us
  blocking collectives  38.2 us (30%)
  local copies, waits for them, and re-layouts  37.8 us (29%)
  Pallas kernels  21.7 us (17%)
  starting transfers between devices  18.5 us (14%)
  waiting for transfers between devices  10 us (8%)
    all_to_all x1, blocking collectives, local(): back = lax.all_to_all(ret, 'rep', 0, 0)  38.2 us
    unnamed x98, local copies, waits for them, and re-layouts  36.7 us
    pallas_call x3, Pallas kernels, project(): pl.pallas_call(functools.partial(project_kernel, slots, copies, has_befor...  12.8 us
    ppermute x10, waiting for transfers between devices, flip(): return lax.ppermute(x, 'tp', [(i, i ^ k) for i in range(copies)])  10 us
    ppermute x10, starting transfers between devices, flip(): return lax.ppermute(x, 'tp', [(i, i ^ k) for i in range(copies)])  7.48 us
    all_to_all x1, starting transfers between devices, local(): prior = lax.all_to_all(prior_sent, ('rep', 'tp'), 0, 0)  6.28 us
    pallas_call x1, Pallas kernels, time_mix(): pl.pallas_call(functools.partial(mix_kernel, slots, copies, direct), in_s...  6.14 us
    all_to_all x1, starting transfers between devices, local(): got = lax.all_to_all(state_sent, 'rep', 0, 0)  4.78 us
  transfers between devices with their start and end apart: 12, of which 2 were waited for; matrix products, arithmetic and copies ran while one was open for 1% of the time, Pallas kernels for 11%

profile of v1, /device:TPU:0, one launch (start us, length us, event | category | flops | bytes accessed | tf_op | source)
XLA Modules:
  0.0 127.1 jit_solution(10620966230225259212)
XLA Ops:
  0.6 0.5 collective-permute-start
  1.1 1.2 slice_bitcast_fusion
  2.3 2.6 %collective-permute-start.1 = (bf16[128,1024]{1,0:T(8,128)(2,1)S(1)}, bf16[128,1024]{1,0:T(8,128)(2,1)S(1)}, u32[]{:S(2)}, u32[]{:S(2)}) collective-permute-start(bf16[128,1024]{1,0:T(8,128)(2,1)S(1)} %get-tuple-element.37), channel_id=1, source_target_pairs={{0,2},{1,3},{2,0},{3,1},{4,6},{5,7},{6,4},{7,5},{8,10},{9,11},{10,... | collective-permute-start | bytes 786440 | tf_op jit(solution)/shard_map/ppermute | solution.py:613
  4.9 0.1 collective-permute-start.6
  5.0 1.1 copy-done.1
  6.1 1.0 copy-done.14
  7.2 0.8 copy-done.33
  8.0 0.8 copy-done.35
  8.8 0.7 copy-done.36
  9.4 0.7 copy-done.41
  10.1 0.7 copy-done.42
  10.8 1.4 %pack.1 = (bf16[8,16,1024]{2,1,0:T(8,128)(2,1)}, f32[32,8,128]{2,1,0:T(8,128)}, bf16[48,1024]{1,0:T(8,128)(2,1)S(1)}) custom-call(s32[16]{0:T(128)S(1)} %copy-done.36, f32[16,8,1024]{2,1,0:T(8,128)S(1)} %copy-done.14, bf16[16,8,16]{2,1,0:T(8,128)(2,1)S(1)} %copy-done.35, bf16[2,16,1024]{2,1,0:T(8,128)(2,1)S(1)} %copy-done.33, ...), custom_call_target="tpu_custom_call" | custom-call | tf_op jit(solution)/shard_map/pack/pallas_call | solution.py:103
  12.2 6.3 %all-to-all-start = ((f32[32,8,128]{2,1,0:T(8,128)}), f32[32,8,128]{2,1,0:T(8,128)S(1)}, u32[]{:S(2)}, u32[]{:S(2)}) async-start(f32[32,8,128]{2,1,0:T(8,128)} %get-tuple-element.23), calls=%async_computation | async-start | bytes 262144 | tf_op jit(solution)/shard_map/all_to_all | solution.py:632
  18.5 1.8 %collective-permute-start.8 = (bf16[128,1024]{1,0:T(8,128)(2,1)S(1)}, bf16[128,1024]{1,0:T(8,128)(2,1)}, u32[]{:S(2)}, u32[]{:S(2)}) collective-permute-start(bf16[128,1024]{1,0:T(8,128)(2,1)S(1)} %get-tuple-element.36), channel_id=1, source_target_pairs={{0,2},{1,3},{2,0},{3,1},{4,6},{5,7},{6,4},{7,5},{8,10},{9,11},{10,... | collective-permute-start | bytes 786440 | tf_op jit(solution)/shard_map/ppermute | solution.py:613
  20.3 0.4 collective-permute-start.2
  20.7 9.2 %collective-permute-done.5.refs_9_.refs_13_ = bf16[48,1024]{1,0:T(8,128)(2,1)S(1)} collective-permute-done((bf16[48,1024]{1,0:T(8,128)(2,1)S(1)}, bf16[48,1024]{1,0:T(8,128)(2,1)S(1)}, u32[]{:S(2)}, u32[]{:S(2)}) %collective-permute-start.5) | collective-permute-done | bytes 98336 | tf_op jit(solution)/shard_map/ppermute | solution.py:613
  29.9 1.4 %collective-permute-start.4 = (bf16[48,1024]{1,0:T(8,128)(2,1)S(1)}, bf16[48,1024]{1,0:T(8,128)(2,1)S(1)}, u32[]{:S(2)}, u32[]{:S(2)}) collective-permute-start(bf16[48,1024]{1,0:T(8,128)(2,1)S(1)} %get-tuple-element.20.refs_6_.refs_10_.refs_16_), channel_id=1, source_target_pairs={{0,2},{1,3},{2,0},{3,1},{4,6},{5,7},{6,4},{7,5},{8,10},{9,11},{10,... | collective-permute-start | bytes 294920 | tf_op jit(solution)/shard_map/ppermute | solution.py:613
  31.3 0.1 collective-permute-start.7
  31.4 4.8 %all-to-all-start.1 = ((bf16[8,16,1024]{2,1,0:T(8,128)(2,1)}), bf16[8,16,1024]{2,1,0:T(8,128)(2,1)}, u32[]{:S(2)}, u32[]{:S(2)}) async-start(bf16[8,16,1024]{2,1,0:T(8,128)(2,1)} %get-tuple-element.30), calls=%async_computation.1 | async-start | bytes 524288 | tf_op jit(solution)/shard_map/all_to_all | solution.py:631
  36.2 0.1 collective-permute-start.3
  36.3 0.5 collective-permute-start.9
  36.8 0.8 collective-permute-done.3.refs_7_.refs_11_
  37.6 0.0 copy-start
  37.6 3.4 %copy-done = bf16[4096,1024]{1,0:T(8,128)(2,1)S(1)} copy-done((bf16[4096,1024]{1,0:T(8,128)(2,1)S(1)}, bf16[4096,1024]{1,0:T(8,128)(2,1)}, u32[]{:S(2)}) %copy-start) | copy-done | bytes 8388632
  41.0 1.1 copy-done.2
  42.1 1.2 copy-done.3
  43.3 0.9 copy-done.5
  44.3 0.7 copy-done.34
  45.0 0.7 copy-done.37
  45.6 0.7 copy-done.39
  46.3 3.7 %project_0.1 = (bf16[128,1024]{1,0:T(8,128)(2,1)S(1)}, f32[128,1024]{1,0:T(8,128)S(1)}) custom-call(s32[16]{0:T(128)S(1)} %copy-done.37, s32[16]{0:T(128)S(1)} %copy-done.39, bf16[384,1024]{1,0:T(8,128)(2,1)S(1)} %bitcast.24, bf16[384,1024]{1,0:T(8,128)(2,1)S(1)} %collective-permute-done.refs_3_.refs_7_, ...), custom_call_target="tpu_custom_call" | custom-call | flops 1073741824 | bytes 8388608 | tf_op jit(solution)/shard_map/project_0/pallas_call | solution.py:253
  50.0 0.7 copy-done.8
  50.7 0.6 copy-done.10
  51.3 0.8 copy-done.15
  52.1 0.7 copy-done.21
  52.8 1.1 copy-done.7
  53.9 1.5 %copy-done.9 = bf16[128,1024]{1,0:T(8,128)(2,1)S(1)} copy-done((bf16[128,1024]{1,0:T(8,128)(2,1)S(1)}, bf16[128,1024]{1,0:T(8,128)(2,1)}, u32[]{:S(2)}) %copy-start.9) | copy-done | bytes 262168
  55.4 0.9 copy-done.11
  56.3 3.7 %project_1.1 = (bf16[128,1024]{1,0:T(8,128)(2,1)S(1)}, f32[128,1024]{1,0:T(8,128)S(1)}) custom-call(s32[16]{0:T(128)S(1)} %copy-done.37, s32[16]{0:T(128)S(1)} %copy-done.39, bf16[384,1024]{1,0:T(8,128)(2,1)S(1)} %bitcast.25, bf16[384,1024]{1,0:T(8,128)(2,1)S(1)} %collective-permute-done.refs_3_.refs_7_, ...), custom_call_target="tpu_custom_call" | custom-call | flops 1073741824 | bytes 8388608 | tf_op jit(solution)/shard_map/project_1/pallas_call | solution.py:253
  60.0 0.0 copy-start.17
  60.0 0.8 copy-done.17
  60.8 0.7 copy-done.23
  61.5 0.0 copy-start.44
  61.6 5.4 %project_2.1 = (bf16[128,1024]{1,0:T(8,128)(2,1)S(1)}, f32[128,1024]{1,0:T(8,128)S(1)}, bf16[48,1024]{1,0:T(8,128)(2,1)S(1)}, f32[48,1024]{1,0:T(8,128)S(1)}) custom-call(s32[16]{0:T(128)S(1)} %copy-done.37, s32[16]{0:T(128)S(1)} %copy-done.39, bf16[384,1024]{1,0:T(8,128)(2,1)S(1)} %bitcast.27, bf16[384,1024]{1,0:T(8,128)(2,1)S(1)} %collective-permute-done.refs_3_.refs_7_, ...), custom_call_target="tpu_custom_call" | custom-call | flops 1476395008 | bytes 8388608 | tf_op jit(solution)/shard_map/project_2/pallas_call | solution.py:253
  67.0 0.8 copy-done.19
  67.8 0.7 copy-done.25
  68.5 0.7 copy-done.27
  69.2 0.6 copy-done.29
  69.9 0.0 copy-start.12
  69.9 1.1 copy-done.12
  71.0 1.1 copy-done.13
  72.2 1.0 copy-done.16
  73.2 1.0 copy-done.18
  74.3 1.0 copy-done.20
  75.3 0.9 copy-done.22
  76.3 0.9 copy-done.24
  77.2 0.9 copy-done.26
  78.2 0.9 copy-done.28
  79.1 0.9 copy-done.30
  80.0 0.8 copy-done.32
  80.8 0.7 copy-done.46
  81.5 6.1 %time_mix.1 = (bf16[384,1024]{1,0:T(8,128)(2,1)}, bf16[32,1024]{1,0:T(8,128)(2,1)}, bf16[8,16,1152]{2,1,0:T(8,128)(2,1)S(1)}) custom-call(s32[16]{0:T(128)S(1)} %copy-done.38, s32[16]{0:T(128)S(1)} %copy-done.40, s32[16]{0:T(128)S(1)} %copy-done.46, bf16[128,1024]{1,0:T(8,128)(2,1)S(1)} %copy-done.22, bf16[128,1024]{1,0:T(8,128)(2,1)S(1)} %copy-done.24, ...), custom_call_target="tpu_custom_call" | custom-call | tf_op jit(solution)/shard_map/time_mix/pallas_call | solution.py:535
  87.6 38.2 %all_to_all.15.back = bf16[8,16,1152]{2,1,0:T(8,128)(2,1)S(1)} all-to-all(bf16[8,16,1152]{2,1,0:T(8,128)(2,1)S(1)} %get-tuple-element.33), channel_id=1, replica_groups=mesh['rep'=8,'tp'=4] {'rep'}, dimensions={0} | all-to-all | bytes 589824 | tf_op jit(solution)/shard_map/all_to_all | solution.py:676
  125.8 1.4 %unpack.1 = (f32[16,8,1024]{2,1,0:T(8,128)}, bf16[16,8,16]{2,1,0:T(8,128)(2,1)}) custom-call(s32[16]{0:T(128)S(1)} %copy-done.38, bf16[8,16,1152]{2,1,0:T(8,128)(2,1)S(1)} %all_to_all.15.back), custom_call_target="tpu_custom_call" | custom-call | tf_op jit(solution)/shard_map/unpack/pallas_call | solution.py:569
  (67 shorter events, 0.1 us)
Async XLA Ops:
  0.6 36.9 %collective-permute-start = (bf16[384,1024]{1,0:T(8,128)(2,1)}, bf16[384,1024]{1,0:T(8,128)(2,1)S(1)}, u32[]{:S(2)}, u32[]{:S(2)}) collective-permute-start(bf16[384,1024]{1,0:T(8,128)(2,1)} %bitcast.21), channel_id=1, source_target_pairs={{0,1},{1,0},{2,3},{3,2},{4,5},{5,4},{6,7},{7,6},{8,9},{9,8},{10,11... | collective-permute-start | bytes 2359304 | tf_op jit(solution)/shard_map/ppermute | solution.py:613
  2.3 18.0 %collective-permute-start.1 = (bf16[128,1024]{1,0:T(8,128)(2,1)S(1)}, bf16[128,1024]{1,0:T(8,128)(2,1)S(1)}, u32[]{:S(2)}, u32[]{:S(2)}) collective-permute-start(bf16[128,1024]{1,0:T(8,128)(2,1)S(1)} %get-tuple-element.37), channel_id=1, source_target_pairs={{0,2},{1,3},{2,0},{3,1},{4,6},{5,7},{6,4},{7,5},{8,10},{9,11},{10,... | collective-permute-start | bytes 786440 | tf_op jit(solution)/shard_map/ppermute | solution.py:613
  4.9 26.4 %collective-permute-start.6 = (bf16[128,1024]{1,0:T(8,128)(2,1)S(1)}, bf16[128,1024]{1,0:T(8,128)(2,1)S(1)}, u32[]{:S(2)}, u32[]{:S(2)}) collective-permute-start(bf16[128,1024]{1,0:T(8,128)(2,1)S(1)} %get-tuple-element.38), channel_id=1, source_target_pairs={{0,2},{1,3},{2,0},{3,1},{4,6},{5,7},{6,4},{7,5},{8,10},{9,11},{10,... | collective-permute-start | bytes 786440 | tf_op jit(solution)/shard_map/ppermute | solution.py:613
  5.0 1.1 copy-start.1
  6.1 1.0 copy-start.14
  7.2 0.8 copy-start.33
  8.0 0.8 copy-start.35
  8.8 0.7 copy-start.36
  9.4 0.7 copy-start.41
  10.1 0.7 copy-start.42
  12.2 19.2 %all-to-all-start = ((f32[32,8,128]{2,1,0:T(8,128)}), f32[32,8,128]{2,1,0:T(8,128)S(1)}, u32[]{:S(2)}, u32[]{:S(2)}) async-start(f32[32,8,128]{2,1,0:T(8,128)} %get-tuple-element.23), calls=%async_computation | async-start | bytes 262144 | tf_op jit(solution)/shard_map/all_to_all | solution.py:632
  18.5 17.9 %collective-permute-start.8 = (bf16[128,1024]{1,0:T(8,128)(2,1)S(1)}, bf16[128,1024]{1,0:T(8,128)(2,1)}, u32[]{:S(2)}, u32[]{:S(2)}) collective-permute-start(bf16[128,1024]{1,0:T(8,128)(2,1)S(1)} %get-tuple-element.36), channel_id=1, source_target_pairs={{0,2},{1,3},{2,0},{3,1},{4,6},{5,7},{6,4},{7,5},{8,10},{9,11},{10,... | collective-permute-start | bytes 786440 | tf_op jit(solution)/shard_map/ppermute | solution.py:613
  20.3 9.6 %collective-permute-start.5 = (bf16[48,1024]{1,0:T(8,128)(2,1)S(1)}, bf16[48,1024]{1,0:T(8,128)(2,1)S(1)}, u32[]{:S(2)}, u32[]{:S(2)}) collective-permute-start(bf16[48,1024]{1,0:T(8,128)(2,1)S(1)} %get-tuple-element.20.refs_6_.refs_10_.refs_16_), channel_id=1, source_target_pairs={{0,3},{1,2},{2,1},{3,0},{4,7},{5,6},{6,5},{7,4},{8,11},{9,10},{10,... | collective-permute-start | bytes 294920 | tf_op jit(solution)/shard_map/ppermute | solution.py:613
  20.3 17.3 %copy-start.6 = (bf16[128,1024]{1,0:T(8,128)(2,1)}, bf16[128,1024]{1,0:T(8,128)(2,1)S(1)}, u32[]{:S(2)}) copy-start(bf16[128,1024]{1,0:T(8,128)(2,1)S(1)} %collective-permute-done.1.refs_4_.refs_8_) | copy-start | bytes 786436
  20.3 17.3 %collective-permute-start.2 = (bf16[128,1024]{1,0:T(8,128)(2,1)S(1)}, bf16[128,1024]{1,0:T(8,128)(2,1)S(1)}, u32[]{:S(2)}, u32[]{:S(2)}) collective-permute-start(bf16[128,1024]{1,0:T(8,128)(2,1)S(1)} %collective-permute-done.1.refs_4_.refs_8_), channel_id=1, source_target_pairs={{0,1},{1,0},{2,3},{3,2},{4,5},{5,4},{6,7},{7,6},{8,9},{9,8},{10,11... | collective-permute-start | bytes 786440 | tf_op jit(solution)/shard_map/ppermute | solution.py:613
  29.9 6.3 %collective-permute-start.4 = (bf16[48,1024]{1,0:T(8,128)(2,1)S(1)}, bf16[48,1024]{1,0:T(8,128)(2,1)S(1)}, u32[]{:S(2)}, u32[]{:S(2)}) collective-permute-start(bf16[48,1024]{1,0:T(8,128)(2,1)S(1)} %get-tuple-element.20.refs_6_.refs_10_.refs_16_), channel_id=1, source_target_pairs={{0,2},{1,3},{2,0},{3,1},{4,6},{5,7},{6,4},{7,5},{8,10},{9,11},{10,... | collective-permute-start | bytes 294920 | tf_op jit(solution)/shard_map/ppermute | solution.py:613
  31.3 21.4 %collective-permute-start.7 = (bf16[128,1024]{1,0:T(8,128)(2,1)S(1)}, bf16[128,1024]{1,0:T(8,128)(2,1)S(1)}, u32[]{:S(2)}, u32[]{:S(2)}) collective-permute-start(bf16[128,1024]{1,0:T(8,128)(2,1)S(1)} %collective-permute-done.6.refs_4_.refs_8_), channel_id=1, source_target_pairs={{0,1},{1,0},{2,3},{3,2},{4,5},{5,4},{6,7},{7,6},{8,9},{9,8},{10,11... | collective-permute-start | bytes 786440 | tf_op jit(solution)/shard_map/ppermute | solution.py:613
  31.4 38.4 %all-to-all-start.1 = ((bf16[8,16,1024]{2,1,0:T(8,128)(2,1)}), bf16[8,16,1024]{2,1,0:T(8,128)(2,1)}, u32[]{:S(2)}, u32[]{:S(2)}) async-start(bf16[8,16,1024]{2,1,0:T(8,128)(2,1)} %get-tuple-element.30), calls=%async_computation.1 | async-start | bytes 524288 | tf_op jit(solution)/shard_map/all_to_all | solution.py:631
  36.2 1.4 %collective-permute-start.3 = (bf16[48,1024]{1,0:T(8,128)(2,1)S(1)}, bf16[48,1024]{1,0:T(8,128)(2,1)S(1)}, u32[]{:S(2)}, u32[]{:S(2)}) collective-permute-start(bf16[48,1024]{1,0:T(8,128)(2,1)S(1)} %get-tuple-element.20.refs_6_.refs_10_.refs_16_), channel_id=1, source_target_pairs={{0,1},{1,0},{2,3},{3,2},{4,5},{5,4},{6,7},{7,6},{8,9},{9,8},{10,11... | collective-permute-start | bytes 294920 | tf_op jit(solution)/shard_map/ppermute | solution.py:613
  36.3 25.2 %collective-permute-start.9 = (bf16[128,1024]{1,0:T(8,128)(2,1)}, bf16[128,1024]{1,0:T(8,128)(2,1)S(1)}, u32[]{:S(2)}, u32[]{:S(2)}) collective-permute-start(bf16[128,1024]{1,0:T(8,128)(2,1)} %collective-permute-done.8.refs_4_), channel_id=1, source_target_pairs={{0,1},{1,0},{2,3},{3,2},{4,5},{5,4},{6,7},{7,6},{8,9},{9,8},{10,11... | collective-permute-start | bytes 786440 | tf_op jit(solution)/shard_map/ppermute | solution.py:613
  37.6 3.4 %copy-start = (bf16[4096,1024]{1,0:T(8,128)(2,1)S(1)}, bf16[4096,1024]{1,0:T(8,128)(2,1)}, u32[]{:S(2)}) copy-start(bf16[4096,1024]{1,0:T(8,128)(2,1)} %refs_17_.3) | copy-start | bytes 25165828
  41.0 1.1 copy-start.2
  42.1 1.2 copy-start.3
  43.3 0.9 copy-start.5
  44.3 0.7 copy-start.34
  45.0 0.7 copy-start.37
  45.6 0.7 copy-start.39
  46.3 15.3 %slice-start = ((s8[8388608]{0:T(1024)(128)(4,1)}), s8[4194304]{0:T(1024)(128)(4,1)S(1)}, s32[]{:S(2)}) async-start(s8[8388608]{0:T(1024)(128)(4,1)} %bitcast.19), calls=%async_computation.3 | async-start | bytes 8388608
  50.0 0.7 copy-start.8
  50.7 0.6 copy-start.10
  51.3 0.8 copy-start.15
  52.1 0.7 copy-start.21
  52.8 8.8 %slice-start.1 = ((s8[8388608]{0:T(1024)(128)(4,1)}), s8[4194304]{0:T(1024)(128)(4,1)S(1)}, s32[]{:S(2)}) async-start(s8[8388608]{0:T(1024)(128)(4,1)} %bitcast.19), calls=%async_computation.4 | async-start | bytes 8388608
  52.8 8.8 %copy-start.4 = (bf16[4096,128]{1,0:T(8,128)(2,1)S(1)}, bf16[4096,128]{1,0:T(8,128)(2,1)}, u32[]{:S(2)}) copy-start(bf16[4096,128]{1,0:T(8,128)(2,1)} %refs_14_.3) | copy-start | bytes 3145732
  52.8 1.1 copy-start.7
  53.9 1.5 %copy-start.9 = (bf16[128,1024]{1,0:T(8,128)(2,1)S(1)}, bf16[128,1024]{1,0:T(8,128)(2,1)}, u32[]{:S(2)}) copy-start(bf16[128,1024]{1,0:T(8,128)(2,1)} %copy-done.8) | copy-start | bytes 786436
  55.4 0.9 copy-start.11
  60.0 0.8 copy-start.17
  60.8 0.7 copy-start.23
  61.5 8.4 %copy-start.31 = (bf16[2,16,1024]{2,1,0:T(8,128)(2,1)S(1)}, bf16[2,16,1024]{2,1,0:T(8,128)(2,1)}, u32[]{:S(2)}) copy-start(bf16[2,16,1024]{2,1,0:T(8,128)(2,1)} %param.24) | copy-start | bytes 196612
  61.5 8.4 %copy-start.38 = (s32[16]{0:T(128)S(1)}, s32[16]{0:T(128)}, u32[]{:S(2)}) copy-start(s32[16]{0:T(128)} %owner.3) | copy-start | bytes 196
  61.5 8.4 %copy-start.40 = (s32[16]{0:T(128)S(1)}, s32[16]{0:T(128)}, u32[]{:S(2)}) copy-start(s32[16]{0:T(128)} %refs_1_.7) | copy-start | bytes 196
  61.5 8.4 %copy-start.43 = (f32[1024]{0:T(1024)S(1)}, f32[1024]{0:T(1024)}, u32[]{:S(2)}) copy-start(f32[1024]{0:T(1024)} %param.30) | copy-start | bytes 12292
  61.5 8.4 %copy-start.44 = (f32[1024]{0:T(1024)S(1)}, f32[1024]{0:T(1024)}, u32[]{:S(2)}) copy-start(f32[1024]{0:T(1024)} %param.33) | copy-start | bytes 12292
  61.5 8.4 %copy-start.45 = (f32[1024]{0:T(1024)S(1)}, f32[1024]{0:T(1024)}, u32[]{:S(2)}) copy-start(f32[1024]{0:T(1024)} %param.34) | copy-start | bytes 12292
  67.0 0.8 copy-start.19
  67.8 0.7 copy-start.25
  68.5 0.7 copy-start.27
  69.2 0.6 copy-start.29
  69.9 1.1 copy-start.12
  71.0 1.1 copy-start.13
  72.2 1.0 copy-start.16
  73.2 1.0 copy-start.18
  74.3 1.0 copy-start.20
  75.3 0.9 copy-start.22
  76.3 0.9 copy-start.24
  77.2 0.9 copy-start.26
  78.2 0.9 copy-start.28
  79.1 0.9 copy-start.30
  80.0 0.8 copy-start.32
  80.8 0.7 copy-start.46
